TPU v7x, 32 devices: a whole 2x2x4 slice. The times are simulated.
32 devices in a mesh: grp: 1, tm: 8 (over y, x, core), op: 4 (over z).
Axes of the slice: x: 2, y: 2, z: 4, core: 2. Of those that a mesh axis runs over, the one named last changes fastest.
Arguments:
- sources: bfloat16 [8, 16, 2, 384, 384], P(('grp', 'tm'), 'op'), may hold values from -6 to 6
- sink: bfloat16 [8, 2, 384, 384], P(('grp', 'tm')), may hold values from -0.3125 to 0.3125
- phase: float32 [8, 384], replicated, may hold values from -3.140625 to 3.140625
- task_table: int32 [3, 8, 16], P(None, ('grp', 'tm'), 'op'), may hold values from -1 to 15, as said below
Outputs:
- task_values: float32 [8, 16, 2, 384], P(('grp', 'tm'), 'op')
Inputs may be any that keep to these rules, and one draw needn't show every extreme that they name: `task_table`: field 0 lies in 0 to 15, field 1 in 0 to 7, field 2 is -1 (dead slot) or a rank 0 to 1. At each time slice, for every owner s exactly 2 homes have slot s live, and their places are 0 to 1, each once. At each time slice one home has all 4 slots live.
All inputs are finite; a program needn't handle non-finite values.
Results may differ from a plain program's by a relative error of at most 0.004.
Values may be sent and summed in bfloat16 or wider, within the bound.
A program may use at most 64 MiB of HBM per device.

v0:
```python
import jax
import jax.numpy as jnp
from jax import lax
from jax.sharding import PartitionSpec as P

SEPARATIONS = (-2, -1, 1, 2)


def shifted_2(shard, axis, by):
    length = lax.axis_size(axis)
    return lax.ppermute(shard, axis, [(i, (i + by) % length) for i in range(length)])


def task_value(source, angle, sink_slice):
    blocks = jnp.einsum("xij,yjl->xyil", source, sink_slice, preferred_element_type=jnp.float32)
    quark_real = blocks[0, 0] - blocks[1, 1]
    quark_imag = blocks[0, 1] + blocks[1, 0]
    cosine = jnp.cos(angle)[None, :]
    sine = jnp.sin(angle)[None, :]
    phased = jnp.stack(
        [quark_real * cosine - quark_imag * sine, quark_real * sine + quark_imag * cosine]
    )
    phased = phased.astype(jnp.bfloat16)
    second = jnp.einsum("xil,yjl->xyij", phased, sink_slice, preferred_element_type=jnp.float32)
    loop_real = second[0, 0] + second[1, 1]
    loop_imag = second[1, 0] - second[0, 1]
    diag_real = jnp.sum(loop_real * loop_real.T - loop_imag * loop_imag.T, axis=1)
    diag_imag = jnp.sum(loop_real * loop_imag.T + loop_imag * loop_real.T, axis=1)
    return jnp.stack([diag_real, diag_imag]) / loop_real.shape[0]


def contract(chosen, angles, sink_slice):

    def single(pair):
        return task_value(pair[0], pair[1], sink_slice)

    return lax.map(single, (chosen, angles))


def angle_rows(moment_values, phase):
    levels = jnp.arange(phase.shape[0], dtype=jnp.float32)
    onehot = (moment_values[:, None] == levels[None, :]).astype(jnp.float32)
    return jnp.dot(
        onehot, phase, precision=lax.Precision.HIGHEST, preferred_element_type=jnp.float32
    )


def shards(sources, sink, phase, task_table):
    slab = sources[0]
    sink_slice = sink[0]
    shifted = {}
    for direction in (1, -1):
        current = slab
        for distance in (1, 2):
            current = shifted_2(current, "tm", -direction)
            shifted[direction * distance] = current
    stacked = jnp.concatenate([shifted[offset] for offset in SEPARATIONS], axis=0)
    picks = task_table[0, 0]
    moments = task_table[1, 0]
    places = task_table[2, 0]
    chosen = jnp.take(stacked, picks, axis=0)
    angles = angle_rows(moments.astype(jnp.float32), phase)
    live = (places >= 0).astype(jnp.float32)
    values = contract(chosen, angles, sink_slice) * live[:, None, None]
    return values[None]


def solution(mesh):
    return jax.shard_map(
        shards,
        mesh=mesh,
        in_specs=(
            P(("grp", "tm"), "op", None, None, None),
            P(("grp", "tm"), None, None, None),
            P(),
            P(None, ("grp", "tm"), "op"),
        ),
        out_specs=P(("grp", "tm"), "op", None, None),
        check_vma=False,
    )
```

profile of v0, /device:TPU:1, one launch (start us, length us, event | category | flops | bytes accessed | tf_op | source)
XLA Modules:
  0.0 148.4 jit_solution(13922783928232581761)
XLA Ops:
  0.0 2.6 %collective-permute-start = (bf16[4,2,384,384]{3,2,1,0:T(8,128)(2,1)}, bf16[4,2,384,384]{3,2,1,0:T(8,128)(2,1)S(1)}, u32[]{:S(2)}, u32[]{:S(2)}) collective-permute-start(bf16[4,2,384,384]{3,2,1,0:T(8,128)(2,1)} %bitcast.95), channel_id=1, source_target_pairs={{0,4},{4,8},{8,12},{12,16},{16,20},{20,24},{24,28},{28,0},{1,5},{5... | collective-permute-start | bytes 7077896 | tf_op jit(solution)/shard_map/ppermute | solution.py:11
  2.6 50.3 %collective-permute-done = bf16[4,2,384,384]{3,2,1,0:T(8,128)(2,1)S(1)} collective-permute-done((bf16[4,2,384,384]{3,2,1,0:T(8,128)(2,1)}, bf16[4,2,384,384]{3,2,1,0:T(8,128)(2,1)S(1)}, u32[]{:S(2)}, u32[]{:S(2)}) %collective-permute-start) | collective-permute-done | bytes 2359328 | tf_op jit(solution)/shard_map/ppermute | solution.py:11
  53.0 2.4 %collective-permute-start.1 = (bf16[4,2,384,384]{3,2,1,0:T(8,128)(2,1)S(1)}, bf16[4,2,384,384]{3,2,1,0:T(8,128)(2,1)}, u32[]{:S(2)}, u32[]{:S(2)}) collective-permute-start(bf16[4,2,384,384]{3,2,1,0:T(8,128)(2,1)S(1)} %collective-permute-done), channel_id=1, source_target_pairs={{0,4},{4,8},{8,12},{12,16},{16,20},{20,24},{24,28},{28,0},{1,5},{5... | collective-permute-start | bytes 7077896 | tf_op jit(solution)/shard_map/ppermute | solution.py:11
  55.3 0.3 collective-permute-done.2
  55.6 0.7 fusion.19
  56.3 0.7 compare_and_fusion
  57.0 0.7 convert_bitcast_fusion
  57.6 0.7 fusion.18
  58.3 0.8 fusion.16
  59.1 45.0 %collective-permute-done.1 = bf16[4,2,384,384]{3,2,1,0:T(8,128)(2,1)} collective-permute-done((bf16[4,2,384,384]{3,2,1,0:T(8,128)(2,1)S(1)}, bf16[4,2,384,384]{3,2,1,0:T(8,128)(2,1)}, u32[]{:S(2)}, u32[]{:S(2)}) %collective-permute-start.1) | collective-permute-done | bytes 2359328 | tf_op jit(solution)/shard_map/ppermute | solution.py:11
  104.1 5.2 %collective-permute-done.3 = bf16[4,2,384,384]{3,2,1,0:T(8,128)(2,1)} collective-permute-done((bf16[4,2,384,384]{3,2,1,0:T(8,128)(2,1)}, bf16[4,2,384,384]{3,2,1,0:T(8,128)(2,1)}, u32[]{:S(2)}, u32[]{:S(2)}) %collective-permute-start.3) | collective-permute-done | bytes 2359328 | tf_op jit(solution)/shard_map/ppermute | solution.py:11
  109.3 8.4 %pad_maximum_fusion = bf16[16,2,384,384]{3,2,1,0:T(8,128)(2,1)} fusion(bf16[4,2,384,384]{3,2,1,0:T(8,128)(2,1)} %collective-permute-done.3, bf16[4,2,384,384]{3,2,1,0:T(8,128)(2,1)} %collective-permute-done.2, bf16[4,2,384,384]{3,2,1,0:T(8,128)(2,1)S(1)} %collective-permute-done, bf16[4,2,384,384]{3,2,1,0:T(8,128)(2,1)} %collective-permute-done.1), kind=kLoop, calls=%fused_computation.34 | loop fusion | flops 14155776 | bytes 18874368 | tf_op jit(solution)/shard_map/concatenate | solution.py:57
  117.6 4.7 %gather_fusion = bf16[4,2,384,384]{3,2,1,0:T(8,128)(2,1)S(1)} fusion(bf16[16,2,384,384]{3,2,1,0:T(8,128)(2,1)} %pad_maximum_fusion, s32[1024]{0:T(1024)S(1)} %pad_clamp_fusion), kind=kCustom, calls=%fused_computation | custom fusion | bytes 4718608 | tf_op jit(solution)/shard_map/jit(_take)/gather | solution.py:61
  122.4 1.7 %broadcast_select_fusion = bf16[4,2,384,384]{3,2,1,0:T(8,128)(2,1)} fusion(bf16[4,2,384,384]{3,2,1,0:T(8,128)(2,1)S(1)} %gather_fusion, pred[4]{0:T(512)(128)(4,1)S(1)} %compare_and_fusion), kind=kLoop, calls=%fused_computation.35 | loop fusion | flops 1179648 | bytes 4718596 | tf_op jit(solution)/shard_map/jit(_take)/select_n | solution.py:61
  124.2 22.9 %while.10 = (s32[]{:T(128)}, f32[4,2,384]{2,1,0:T(2,128)}, bf16[4,2,384,384]{3,2,1,0:T(8,128)(2,1)}, bf16[2,384,384]{2,1,0:T(8,128)(2,1)S(1)}, f32[4,384]{1,0:T(4,128)}, /*index=5*/s32[]{:T(128)}) while((s32[]{:T(128)}, f32[4,2,384]{2,1,0:T(2,128)}, bf16[4,2,384,384]{3,2,1,0:T(8,128)(2,1)}, bf16[2,384,384]{2,1,0:T(8,128)(2,1)S(1)}, ...), condition=%wide.region_3.4_spmd, body=%wide.region_0.3_spmd.sunk | while | flops 910246656 | bytes 23617096 | solution.py:37
  124.2 1.8 %convolution_bitcast_fusion.4 = f32[2,2,384,384]{3,2,1,0:T(8,128)S(1)} fusion(bf16[2,384,384]{2,1,0:T(8,128)(2,1)S(1)} %get-tuple-element.116, bf16[4,2,384,384]{3,2,1,0:T(8,128)(2,1)} %get-tuple-element.115, s32[]{:T(128)} %get-tuple-element.107), kind=kOutput, calls=%fused_computation.2.clone.1 | convolution fusion | flops 452984832 | bytes 3539456 | tf_op jit(solution)/shard_map/while/body/eval_jaxpr/xij,yjl->xyil/dot_general | solution.py:15
  126.0 0.8 cosine_reduce_fusion.2
  126.8 0.2 subtract_convert_fusion.2
  127.0 0.8 convolution_bitcast_fusion.5
  127.8 0.1 fusion.30
  127.9 0.2 copy.18
  128.2 0.2 copy.19
  128.4 0.1 add_bitcast_fusion.2
  128.5 0.2 copy.20
  128.7 0.2 copy.21
  128.9 0.3 fusion.31
  129.3 0.6 fusion.32
  129.9 1.8 %convolution_bitcast_fusion.4 = f32[2,2,384,384]{3,2,1,0:T(8,128)S(1)} fusion(bf16[2,384,384]{2,1,0:T(8,128)(2,1)S(1)} %get-tuple-element.116, bf16[4,2,384,384]{3,2,1,0:T(8,128)(2,1)} %get-tuple-element.115, s32[]{:T(128)} %get-tuple-element.107), kind=kOutput, calls=%fused_computation.2.clone.1 | convolution fusion | flops 452984832 | bytes 3539456 | tf_op jit(solution)/shard_map/while/body/eval_jaxpr/xij,yjl->xyil/dot_general | solution.py:15
  131.7 0.8 cosine_reduce_fusion.2
  132.5 0.2 subtract_convert_fusion.2
  132.7 0.8 convolution_bitcast_fusion.5
  133.5 0.1 fusion.30
  133.6 0.2 copy.18
  133.9 0.2 copy.19
  134.1 0.1 add_bitcast_fusion.2
  134.2 0.2 copy.20
  134.4 0.2 copy.21
  134.7 0.3 fusion.31
  135.0 0.6 fusion.32
  135.6 1.8 %convolution_bitcast_fusion.4 = f32[2,2,384,384]{3,2,1,0:T(8,128)S(1)} fusion(bf16[2,384,384]{2,1,0:T(8,128)(2,1)S(1)} %get-tuple-element.116, bf16[4,2,384,384]{3,2,1,0:T(8,128)(2,1)} %get-tuple-element.115, s32[]{:T(128)} %get-tuple-element.107), kind=kOutput, calls=%fused_computation.2.clone.1 | convolution fusion | flops 452984832 | bytes 3539456 | tf_op jit(solution)/shard_map/while/body/eval_jaxpr/xij,yjl->xyil/dot_general | solution.py:15
  137.4 0.8 cosine_reduce_fusion.2
  138.2 0.2 subtract_convert_fusion.2
  138.4 0.8 convolution_bitcast_fusion.5
  139.2 0.1 fusion.30
  139.4 0.2 copy.18
  139.6 0.2 copy.19
  139.8 0.1 add_bitcast_fusion.2
  139.9 0.2 copy.20
  140.1 0.2 copy.21
  140.4 0.3 fusion.31
  140.7 0.6 fusion.32
  141.3 1.8 %convolution_bitcast_fusion.4 = f32[2,2,384,384]{3,2,1,0:T(8,128)S(1)} fusion(bf16[2,384,384]{2,1,0:T(8,128)(2,1)S(1)} %get-tuple-element.116, bf16[4,2,384,384]{3,2,1,0:T(8,128)(2,1)} %get-tuple-element.115, s32[]{:T(128)} %get-tuple-element.107), kind=kOutput, calls=%fused_computation.2.clone.1 | convolution fusion | flops 452984832 | bytes 3539456 | tf_op jit(solution)/shard_map/while/body/eval_jaxpr/xij,yjl->xyil/dot_general | solution.py:15
  143.1 0.8 cosine_reduce_fusion.2
  143.9 0.2 subtract_convert_fusion.2
  144.1 0.8 convolution_bitcast_fusion.5
  144.9 0.1 fusion.30
  145.1 0.2 copy.18
  145.3 0.2 copy.19
  145.6 0.1 add_bitcast_fusion.2
  145.6 0.2 copy.20
  145.9 0.2 copy.21
  146.1 0.3 fusion.31
  146.4 0.6 fusion.32
  147.0 1.4 multiply_bitcast_fusion
  (16 shorter events, 0.1 us)
Async XLA Ops:
  0.0 58.3 %copy-start = (f32[8,384]{1,0:T(8,128)S(1)}, f32[8,384]{1,0:T(8,128)}, u32[]{:S(2)}) copy-start(f32[8,384]{1,0:T(8,128)} %param.8) | copy-start | bytes 36868
  0.0 53.0 %collective-permute-start = (bf16[4,2,384,384]{3,2,1,0:T(8,128)(2,1)}, bf16[4,2,384,384]{3,2,1,0:T(8,128)(2,1)S(1)}, u32[]{:S(2)}, u32[]{:S(2)}) collective-permute-start(bf16[4,2,384,384]{3,2,1,0:T(8,128)(2,1)} %bitcast.95), channel_id=1, source_target_pairs={{0,4},{4,8},{8,12},{12,16},{16,20},{20,24},{24,28},{28,0},{1,5},{5... | collective-permute-start | bytes 7077896 | tf_op jit(solution)/shard_map/ppermute | solution.py:11
  2.6 53.0 %collective-permute-start.2 = (bf16[4,2,384,384]{3,2,1,0:T(8,128)(2,1)}, bf16[4,2,384,384]{3,2,1,0:T(8,128)(2,1)}, u32[]{:S(2)}, u32[]{:S(2)}) collective-permute-start(bf16[4,2,384,384]{3,2,1,0:T(8,128)(2,1)} %bitcast.96), channel_id=1, source_target_pairs={{0,28},{4,0},{8,4},{12,8},{16,12},{20,16},{24,20},{28,24},{1,29},{... | collective-permute-start | bytes 7077896 | tf_op jit(solution)/shard_map/ppermute | solution.py:11
  53.0 51.1 %collective-permute-start.1 = (bf16[4,2,384,384]{3,2,1,0:T(8,128)(2,1)S(1)}, bf16[4,2,384,384]{3,2,1,0:T(8,128)(2,1)}, u32[]{:S(2)}, u32[]{:S(2)}) collective-permute-start(bf16[4,2,384,384]{3,2,1,0:T(8,128)(2,1)S(1)} %collective-permute-done), channel_id=1, source_target_pairs={{0,4},{4,8},{8,12},{12,16},{16,20},{20,24},{24,28},{28,0},{1,5},{5... | collective-permute-start | bytes 7077896 | tf_op jit(solution)/shard_map/ppermute | solution.py:11
  55.6 53.6 %collective-permute-start.3 = (bf16[4,2,384,384]{3,2,1,0:T(8,128)(2,1)}, bf16[4,2,384,384]{3,2,1,0:T(8,128)(2,1)}, u32[]{:S(2)}, u32[]{:S(2)}) collective-permute-start(bf16[4,2,384,384]{3,2,1,0:T(8,128)(2,1)} %collective-permute-done.2), channel_id=1, source_target_pairs={{0,28},{4,0},{8,4},{12,8},{16,12},{20,16},{24,20},{28,24},{1,29},{... | collective-permute-start | bytes 7077896 | tf_op jit(solution)/shard_map/ppermute | solution.py:11
  122.4 1.8 %copy-start.1 = (bf16[1,2,384,384]{3,2,1,0:T(8,128)(2,1)S(1)}, bf16[1,2,384,384]{3,2,1,0:T(8,128)(2,1)}, u32[]{:S(2)}) copy-start(bf16[1,2,384,384]{3,2,1,0:T(8,128)(2,1)} %param.7) | copy-start | bytes 1769476
where the time goes:
time: 149 us; the launch traced here: 148 us
  waiting for transfers between devices  101 us (68%)
  other arithmetic  19.5 us (13%)
  local copies, waits for them, and re-layouts  11.6 us (8%)
  matrix products  11.3 us (8%)
  starting transfers between devices  4.98 us (3%)
    ppermute x4, waiting for transfers between devices, shifted_2(): lax.ppermute(shard, axis, [(i, (i + by) % length) for i in range(length)])  101 us
    concatenate x1, other arithmetic, shards(): jnp.concatenate([shifted[offset] for offset in SEPARATIONS], axis=0)  8.36 us
    dot_general x4, matrix products, task_value(): jnp.einsum('xij,yjl->xyil', source, sink_slice, preferred_element_type=jn...  7.35 us
    ppermute x4, starting transfers between devices, shifted_2(): lax.ppermute(shard, axis, [(i, (i + by) % length) for i in range(length)])  4.98 us
    gather x1, local copies, waits for them, and re-layouts, shards(): chosen = jnp.take(stacked, picks, axis=0)  4.75 us
    dot_general x4, matrix products, task_value(): jnp.einsum('xil,yjl->xyij', phased, sink_slice, preferred_element_type=jn...  3.2 us
    cos x4, local copies, waits for them, and re-layouts, task_value(): cosine = jnp.cos(angle)[None, :]  3.09 us
  transfers between devices with their start and end apart: 4, of which 4 were waited for; matrix products, arithmetic and copies ran while one was open for 2% of the time, Pallas kernels for 0%

commit v1 on v0

v1 whole, which is shorter than its diff:
```python
import functools

import jax
import jax.numpy as jnp
from jax import lax
from jax.experimental import pallas as pl
from jax.experimental.pallas import tpu as pltpu
from jax.sharding import PartitionSpec as P

SEPARATIONS = (-2, -1, 1, 2)
MESH = pl.DeviceIdType.MESH


def greet(neighbours):
    barrier = pltpu.get_barrier_semaphore()
    for neighbour in neighbours:
        pl.semaphore_signal(barrier, inc=1, device_id={"tm": neighbour}, device_id_type=MESH)
    pl.semaphore_wait(barrier, len(neighbours))


def remote(src, dst, send, recv, neighbour):
    return pltpu.make_async_remote_copy(
        src_ref=src, dst_ref=dst, send_sem=send, recv_sem=recv,
        device_id={"tm": neighbour}, device_id_type=MESH,
    )


def gather_kernel(
    n, pieces, table_ref, sink_ref, sinks_ref, tables_ref,
    own, t_send, t_recv, x_send, x_recv, y_send, y_recv, p_send, p_recv, f_send, f_recv,
):
    me = lax.axis_index("tm")
    slots = table_ref.shape[2]
    chip, core = me // 2, me % 2
    mate = chip * 2 + 1 - core
    relay = n == 8
    neighbours = [(me - d + n) % n for d in SEPARATIONS]
    if relay:
        across = ((chip // 2) * 2 + 1 - chip % 2) * 2 + core
        beside = (me + n // 2) % n
        greet(neighbours + [beside])
    else:
        greet(neighbours)

    rows = sink_ref.shape[0] // pieces

    def part(ref, k):
        return ref.at[pl.ds(k * rows, rows)]

    if relay:
        x_here = 3 * (chip % 2)
        y_here = 3 - x_here
        x_copies = [
            remote(part(sink_ref, k), part(sinks_ref.at[3 - x_here], k), x_send.at[k], x_recv.at[k], across)
            for k in range(pieces)
        ]
        y_copies = [
            remote(part(sinks_ref.at[x_here], k), part(sinks_ref.at[y_here], k), y_send.at[k], y_recv.at[k], beside)
            for k in range(pieces)
        ]
    else:
        x_copies = [
            remote(part(sink_ref, k), part(sinks_ref.at[0], k), x_send.at[k], x_recv.at[k], (me + n - 2) % n)
            for k in range(pieces)
        ]
        y_copies = [
            remote(part(sink_ref, k), part(sinks_ref.at[3], k), y_send.at[k], y_recv.at[k], (me + 2) % n)
            for k in range(pieces)
        ]
    p_copy = remote(sink_ref, sinks_ref.at[2 - core], p_send, p_recv, mate)
    f_copies = [
        remote(part(sinks_ref.at[3 * core], k), part(sinks_ref.at[1 + core], k), f_send.at[k], f_recv.at[k], mate)
        for k in range(pieces)
    ]

    for copy in x_copies:
        copy.start()
    if not relay:
        for copy in y_copies:
            copy.start()
    p_copy.start()

    row = lax.broadcasted_iota(jnp.int32, own.shape, 0)
    lane = lax.broadcasted_iota(jnp.int32, own.shape, 1)
    packed = jnp.zeros(own.shape, jnp.int32)
    for f in range(3):
        for s in range(slots):
            packed = jnp.where((row == f) & (lane == s), table_ref[f, 0, s], packed)
    own[...] = packed
    t_copies = [
        remote(own, tables_ref.at[o], t_send.at[o], t_recv.at[o], (me + d + n) % n)
        for o, d in enumerate(SEPARATIONS)
    ]
    for copy in t_copies:
        copy.start()

    for k in range(pieces):
        x_copies[k].wait_recv()
        if relay:
            y_copies[k].start()

            @pl.when(3 * core == x_here)
            def _():
                f_copies[k].start()
        else:
            @pl.when(core == 0)
            def _():
                f_copies[k].start()
    for k in range(pieces):
        y_copies[k].wait_recv()
        if relay:
            @pl.when(3 * core != x_here)
            def _():
                f_copies[k].start()
        else:
            @pl.when(core == 1)
            def _():
                f_copies[k].start()
    for copy in t_copies:
        copy.wait()
    p_copy.wait()
    for k in range(pieces):
        f_copies[k].wait()
        x_copies[k].wait_send()
        y_copies[k].wait_send()


def task_kernel(
    tables_ref, phase_ref, sources_ref, sinks_ref, out_ref, source, weight, cosine, sine, todo, sems,
):
    offsets, slots = out_ref.shape[:2]
    ops, dim = sources_ref.shape[0], source.shape[1]

    def scan(j, count):
        o, s = j // slots, j % slots
        mine = (tables_ref[o, 2, s] >= 0) & (tables_ref[o, 0, s] // ops == o)

        @pl.when(mine)
        def _():
            todo[count] = j

        return count + mine.astype(jnp.int32)

    count = lax.fori_loop(0, offsets * slots, scan, jnp.int32(0))

    def copies(i):
        j, slot = todo[i], i % 2
        o, s = j // slots, j % slots
        a = tables_ref[o, 0, s] % ops
        first, last = pl.ds(0, dim), pl.ds(dim, dim)
        pairs = (
            (sources_ref.at[a, 0], source.at[slot, :, first]),
            (sources_ref.at[a, 1], source.at[slot, :, last]),
            (sinks_ref.at[o, 0], weight.at[slot, first, first]),
            (sinks_ref.at[o, 0], weight.at[slot, last, last]),
            (sinks_ref.at[o, 1], weight.at[slot, first, last]),
        )
        return [pltpu.make_async_copy(a, b, sems.at[slot, q]) for q, (a, b) in enumerate(pairs)]

    @pl.when(count > 0)
    def _():
        for copy in copies(0):
            copy.start()

    out_ref[...] = jnp.zeros_like(out_ref)
    cosine[...] = jnp.cos(phase_ref[...])
    sine[...] = jnp.sin(phase_ref[...])

    def step(i, carry):
        slot = i % 2
        for copy in copies(i):
            copy.wait()

        @pl.when(i + 1 < count)
        def _():
            for copy in copies(i + 1):
                copy.start()

        j = todo[i]
        o, s = j // slots, j % slots
        moment = tables_ref[o, 1, s]
        weight[slot, dim:, :dim] = -weight[slot, :dim, dim:]
        quark = jnp.dot(source[slot], weight[slot], preferred_element_type=jnp.float32)
        c, z = cosine[pl.ds(moment, 1), :], sine[pl.ds(moment, 1), :]
        real, imag = quark[:, :dim], quark[:, dim:]
        phased = jnp.concatenate([real * c - imag * z, real * z + imag * c], axis=1).astype(jnp.bfloat16)
        loop = lax.dot_general(
            phased, weight[slot], (((1,), (1,)), ((), ())), preferred_element_type=jnp.float32
        )
        real, imag = loop[:, :dim], loop[:, dim:]
        real_t, imag_t = real.T, imag.T
        out_ref[o, s, 0:1] = jnp.sum(real * real_t - imag * imag_t, axis=0, keepdims=True) / dim
        out_ref[o, s, 1:2] = jnp.sum(real * imag_t + imag * real_t, axis=0, keepdims=True) / dim
        return carry

    lax.fori_loop(0, count, step, 0)


def return_kernel(n, values_ref, out_ref, parts, send, recv):
    me = lax.axis_index("tm")
    owners = [(me - d + n) % n for d in SEPARATIONS]
    greet(owners)
    copies = [
        remote(values_ref.at[o], parts.at[o], send.at[o], recv.at[o], owner) for o, owner in enumerate(owners)
    ]
    for copy in copies:
        copy.start()
    for copy in copies:
        copy.wait()
    out_ref[0] = (parts[0] + parts[1]) + (parts[2] + parts[3])


def shards(n, sources, sink, phase, task_table):
    ops, dim = sources.shape[1], sources.shape[-1]
    slots = task_table.shape[2]
    offsets = len(SEPARATIONS)
    pieces = 8 if (2 * dim) % 128 == 0 else 1
    any_spec = pl.BlockSpec(memory_space=pl.ANY)
    smem_spec = pl.BlockSpec(memory_space=pltpu.SMEM)
    vmem_spec = pl.BlockSpec(memory_space=pltpu.VMEM)
    dma = pltpu.SemaphoreType.DMA
    sinks, tables = pl.pallas_call(
        functools.partial(gather_kernel, n, pieces),
        out_shape=(
            jax.ShapeDtypeStruct((offsets, 2 * dim, dim), sink.dtype),
            jax.ShapeDtypeStruct((offsets, 8, 128), jnp.int32),
        ),
        in_specs=[smem_spec, any_spec],
        out_specs=(any_spec, any_spec),
        scratch_shapes=[
            pltpu.VMEM((8, 128), jnp.int32),
            dma((offsets,)), dma((offsets,)),
            dma((pieces,)), dma((pieces,)), dma((pieces,)), dma((pieces,)),
            dma, dma, dma((pieces,)), dma((pieces,)),
        ],
        compiler_params=pltpu.CompilerParams(collective_id=0, has_side_effects=True),
        name="gather_sinks",
    )(task_table, sink.reshape(2 * dim, dim))
    values = pl.pallas_call(
        task_kernel,
        out_shape=jax.ShapeDtypeStruct((offsets, slots, 2, dim), jnp.float32),
        in_specs=[smem_spec, vmem_spec, any_spec, any_spec],
        out_specs=vmem_spec,
        scratch_shapes=[
            pltpu.VMEM((2, dim, 2 * dim), sources.dtype),
            pltpu.VMEM((2, 2 * dim, 2 * dim), sources.dtype),
            pltpu.VMEM(phase.shape, jnp.float32),
            pltpu.VMEM(phase.shape, jnp.float32),
            pltpu.SMEM((offsets * slots,), jnp.int32),
            dma((2, 5)),
        ],
        compiler_params=pltpu.CompilerParams(vmem_limit_bytes=40 * 1024 * 1024),
        name="tasks",
    )(tables, phase, sources[0], sinks.reshape(offsets, 2, dim, dim))
    return pl.pallas_call(
        functools.partial(return_kernel, n),
        out_shape=jax.ShapeDtypeStruct((1, slots, 2, dim), jnp.float32),
        in_specs=[vmem_spec],
        out_specs=vmem_spec,
        scratch_shapes=[
            pltpu.VMEM((offsets, slots, 2, dim), jnp.float32),
            dma((offsets,)), dma((offsets,)),
        ],
        compiler_params=pltpu.CompilerParams(collective_id=1, has_side_effects=True),
        name="return_values",
    )(values)


def solution(mesh):
    return jax.shard_map(
        functools.partial(shards, mesh.shape["tm"]),
        mesh=mesh,
        in_specs=(
            P(("grp", "tm"), "op", None, None, None),
            P(("grp", "tm"), None, None, None),
            P(),
            P(None, ("grp", "tm"), "op"),
        ),
        out_specs=P(("grp", "tm"), "op", None, None),
        check_vma=False,
    )
```

time: 149 us -> 47.4 us (0.32)
  the two profiles are of different devices: /device:TPU:1 before, /device:TPU:0 now
where the time goes in v1:
time: 47.4 us; the launch traced here: 48.3 us
  Pallas kernels  41.6 us (88%)
  local copies, waits for them, and re-layouts  6.67 us (14%)
    pallas_call x1, Pallas kernels, shards(): pl.pallas_call(functools.partial(gather_kernel, n, pieces), out_shape=(ja...  23.4 us
    pallas_call x1, Pallas kernels, shards(): pl.pallas_call(functools.partial(return_kernel, n), out_shape=jax.ShapeDt...  9.81 us
    pallas_call x1, Pallas kernels, shards(): pl.pallas_call(task_kernel, out_shape=jax.ShapeDtypeStruct((offsets, slot...  8.38 us
    unnamed x11, local copies, waits for them, and re-layouts  6.67 us

profile of v1, /device:TPU:0, one launch (start us, length us, event | category | flops | bytes accessed | tf_op | source)
XLA Modules:
  0.0 48.3 jit_solution(5303457534509846859)
XLA Ops:
  0.0 23.4 %gather_sinks.1 = (bf16[4,768,384]{2,1,0:T(8,128)(2,1)}, s32[4,8,128]{2,1,0:T(8,128)}) custom-call(s32[3,1,4]{2,1,0:T(1,128)} %table_ref.1, bf16[768,384]{1,0:T(8,128)(2,1)} %bitcast.5), custom_call_target="tpu_custom_call" | custom-call | tf_op jit(solution)/shard_map/gather_sinks/pallas_call | solution.py:222
  23.4 0.0 copy-start
  23.4 1.7 %copy-done = bf16[1,4,2,384,384]{4,3,2,1,0:T(8,128)(2,1)S(1)} copy-done((bf16[1,4,2,384,384]{4,3,2,1,0:T(8,128)(2,1)S(1)}, bf16[1,4,2,384,384]{4,3,2,1,0:T(8,128)(2,1)}, u32[]{:S(2)}) %copy-start) | copy-done | bytes 2359320
  25.0 0.0 copy-start.1
  25.0 1.7 %copy-done.1 = bf16[4,768,384]{2,1,0:T(8,128)(2,1)S(1)} copy-done((bf16[4,768,384]{2,1,0:T(8,128)(2,1)S(1)}, bf16[4,768,384]{2,1,0:T(8,128)(2,1)}, u32[]{:S(2)}) %copy-start.1) | copy-done | bytes 2359320
  26.7 0.0 copy-start.3
  26.7 0.7 %copy-done.3 = s32[4,8,128]{2,1,0:T(8,128)S(1)} copy-done((s32[4,8,128]{2,1,0:T(8,128)S(1)}, s32[4,8,128]{2,1,0:T(8,128)}, u32[]{:S(2)}) %copy-start.3) | copy-done | bytes 16408
  27.4 0.0 copy-start.4
  27.4 0.7 %copy-done.4 = f32[8,384]{1,0:T(8,128)S(1)} copy-done((f32[8,384]{1,0:T(8,128)S(1)}, f32[8,384]{1,0:T(8,128)}, u32[]{:S(2)}) %copy-start.4) | copy-done | bytes 12312
  28.1 8.4 %tasks.1.values_ref = f32[4,4,2,384]{3,2,1,0:T(2,128)S(1)} custom-call(s32[4,8,128]{2,1,0:T(8,128)S(1)} %copy-done.3, f32[8,384]{1,0:T(8,128)S(1)} %copy-done.4, bf16[4,2,384,384]{3,2,1,0:T(8,128)(2,1)S(1)} %bitcast.3, bf16[4,2,384,384]{3,2,1,0:T(8,128)(2,1)S(1)} %bitcast.4), custom_call_target="tpu_custom_call" | custom-call | tf_op jit(solution)/shard_map/tasks/pallas_call | solution.py:239
  36.5 0.0 copy-start.2
  36.5 0.6 %copy-done.2 = f32[4,4,2,384]{3,2,1,0:T(2,128)} copy-done((f32[4,4,2,384]{3,2,1,0:T(2,128)}, f32[4,4,2,384]{3,2,1,0:T(2,128)S(1)}, u32[]{:S(2)}) %copy-start.2) | copy-done | bytes 49176
  37.1 9.8 %return_values.1 = f32[1,4,2,384]{3,2,1,0:T(2,128)} custom-call(f32[4,4,2,384]{3,2,1,0:T(2,128)} %copy-done.2), custom_call_target="tpu_custom_call" | custom-call | tf_op jit(solution)/shard_map/return_values/pallas_call | solution.py:255
  47.0 1.3 %copy.6 = f32[1,4,2,384]{3,2,1,0:T(2,128)} copy(f32[1,4,2,384]{3,2,1,0:T(2,128)} %return_values.1) | data formatting | bytes 24576
Async XLA Ops:
  23.4 1.7 %copy-start = (bf16[1,4,2,384,384]{4,3,2,1,0:T(8,128)(2,1)S(1)}, bf16[1,4,2,384,384]{4,3,2,1,0:T(8,128)(2,1)}, u32[]{:S(2)}) copy-start(bf16[1,4,2,384,384]{4,3,2,1,0:T(8,128)(2,1)} %param.4) | copy-start | bytes 7077892
  25.0 1.7 %copy-start.1 = (bf16[4,768,384]{2,1,0:T(8,128)(2,1)S(1)}, bf16[4,768,384]{2,1,0:T(8,128)(2,1)}, u32[]{:S(2)}) copy-start(bf16[4,768,384]{2,1,0:T(8,128)(2,1)} %get-tuple-element.8) | copy-start | bytes 7077892
  26.7 0.7 %copy-start.3 = (s32[4,8,128]{2,1,0:T(8,128)S(1)}, s32[4,8,128]{2,1,0:T(8,128)}, u32[]{:S(2)}) copy-start(s32[4,8,128]{2,1,0:T(8,128)} %get-tuple-element.7.tables_ref) | copy-start | bytes 49156
  27.4 0.7 %copy-start.4 = (f32[8,384]{1,0:T(8,128)S(1)}, f32[8,384]{1,0:T(8,128)}, u32[]{:S(2)}) copy-start(f32[8,384]{1,0:T(8,128)} %phase_ref.1) | copy-start | bytes 36868
  36.5 0.6 %copy-start.2 = (f32[4,4,2,384]{3,2,1,0:T(2,128)}, f32[4,4,2,384]{3,2,1,0:T(2,128)S(1)}, u32[]{:S(2)}) copy-start(f32[4,4,2,384]{3,2,1,0:T(2,128)S(1)} %tasks.1.values_ref) | copy-start | bytes 147460
